TPU v7x, 128 devices: a whole 4x4x4 slice. The times are simulated.
128 devices in a mesh: ax: 8 (over z, core), circ: 16 (over y, x).
Axes of the slice: x: 4, y: 4, z: 4, core: 2. Of those that a mesh axis runs over, the one named last changes fastest.
Arguments:
- blocks_a: bfloat16 [64, 128, 5, 128, 128], P('ax', 'circ'), may hold values from -0.5 to 0.5
- blocks_p: bfloat16 [64, 128, 3, 128, 128], P('ax', 'circ'), may hold values from -0.5 to 0.5
- send_slot: int32 [64, 128, 3, 5, 3], P('ax', 'circ'), may hold values from 0 to 255, as said below
- recv_entry: int32 [128, 256], P(('ax', 'circ')), may hold values from 0 to 63, as said below
Outputs:
- coarse: bfloat16 [8192, 128, 128], P(('ax', 'circ'))
Inputs may be any that keep to these rules, and one draw needn't show every extreme that they name: `send_slot`: all terms of one block row and one k name the same owner; a few owners are named by far more terms than the rest. `recv_entry`: each row names every value exactly 4 times.
All inputs are finite; a program needn't handle non-finite values.
Results may differ from a plain program's by a relative error of at most 0.0064.
Values may be sent and summed in bfloat16 or wider, within the bound.
A program may use at most 192 MiB of HBM per device.

v0:
```python
import functools

import jax
import jax.numpy as jnp
from jax import lax
from jax.experimental import pallas as pl
from jax.experimental.pallas import tpu as pltpu
from jax.sharding import PartitionSpec as P

MESH = pl.DeviceIdType.MESH
B = 128
ROWS = 64
KP = 3
ST = 5
TASKS = ROWS * KP
OWNERS = 128
ENTRIES = 64
CHUNKS = ((0, 32), (32, 32), (64, 32), (96, 32))
STEP = 37
NT = (((1,), (1,)), ((), ()))
OFF_PERM = TASKS * ST
OFF_SAME = OFF_PERM + TASKS
OFF_LAST = OFF_SAME + TASKS
OFF_SOME = OFF_LAST + OWNERS
OFF_INV = OFF_SOME + OWNERS


def transpose_kernel(x_ref, o_ref):
    for i in range(x_ref.shape[0]):
        o_ref[i] = x_ref[i].T


def transposed(blocks, step):
    count = blocks.shape[0]
    spec = pl.BlockSpec((step, B, B), lambda i: (i, 0, 0))
    return pl.pallas_call(
        transpose_kernel,
        grid=(count // step,),
        out_shape=jax.ShapeDtypeStruct((count, B, B), jnp.bfloat16),
        in_specs=[spec],
        out_specs=spec,
        cost_estimate=pl.CostEstimate(flops=0, bytes_accessed=count * B * B * 4, transcendentals=0),
        compiler_params=pltpu.CompilerParams(vmem_limit_bytes=32 * 2**20),
    )(blocks)


def offset_device(step):
    ax, ci = lax.axis_index("ax"), lax.axis_index("circ")
    off = lax.rem(step * STEP, 128)
    core = lax.rem(ax + off, 2)
    x = lax.rem(lax.rem(ci, 4) + off // 2, 4)
    y = lax.rem(ci // 4 + off // 8, 4)
    z = lax.rem(ax // 2 + off // 32, 4)
    return z * 2 + core, y * 4 + x


def galerkin_kernel(tab, a_hbm, pt_hbm, out_ref, a_buf, px, s_buf, term, run, *rest):
    n_chunks = len(CHUNKS)
    sends, recvs = rest[:n_chunks], rest[n_chunks : 2 * n_chunks]
    a_sem, p_sem, hs_sem, hr_sem, s_sem, r_sem = rest[2 * n_chunks :]
    ax, ci = lax.axis_index("ax"), lax.axis_index("circ")
    me = ax * 16 + ci
    n_ax, n_ci = 8, 16

    a_copy = pltpu.make_async_copy(a_hbm, a_buf, a_sem)
    a_copy.start()
    p_copy = pltpu.make_async_copy(pt_hbm, px.at[pl.ds(1, 8), pl.ds(1, 8)], p_sem)
    p_copy.start()

    barrier = pltpu.get_barrier_semaphore()

    def greet(i, carry):
        pl.semaphore_signal(barrier, inc=1, device_id=offset_device(i), device_id_type=MESH)
        return carry

    lax.fori_loop(1, OWNERS, greet, 0)
    pl.semaphore_wait(barrier, OWNERS - 1)

    up, down = (lax.rem(ax + n_ax - 1, n_ax), ci), (lax.rem(ax + 1, n_ax), ci)
    left, right = (ax, lax.rem(ci + n_ci - 1, n_ci)), (ax, lax.rem(ci + 1, n_ci))
    halos = []
    for h, (c0, cw) in enumerate(CHUNKS):
        cols = pl.ds(c0, cw)
        eight = pl.ds(1, 8)
        four = (
            (pt_hbm.at[:, 0, :, cols], px.at[eight, 9, :, cols], left),
            (pt_hbm.at[:, 7, :, cols], px.at[eight, 0, :, cols], right),
            (pt_hbm.at[0, :, :, cols], px.at[9, eight, :, cols], up),
            (pt_hbm.at[7, :, :, cols], px.at[0, eight, :, cols], down),
        )
        copies = []
        for d, (src, dst, device) in enumerate(four):
            copy = pltpu.make_async_remote_copy(
                src_ref=src,
                dst_ref=dst,
                send_sem=hs_sem.at[h * 4 + d],
                recv_sem=hr_sem.at[h * 4 + d],
                device_id=device,
                device_id_type=MESH,
            )
            copy.start()
            copies.append(copy)
        halos.append(copies)

    p_copy.wait()
    a_copy.wait()

    for h, (c0, cw) in enumerate(CHUNKS):
        send, recv = sends[h], recvs[h]
        cols = pl.ds(c0, cw)
        two = 2 * cw
        for copy in halos[h]:
            copy.wait()

        @pl.when(ax == 0)
        def _():
            px[0, pl.ds(1, 8), :, cols] = jnp.zeros((8, KP, cw, B), jnp.bfloat16)

        @pl.when(ax == n_ax - 1)
        def _():
            px[9, pl.ds(1, 8), :, cols] = jnp.zeros((8, KP, cw, B), jnp.bfloat16)

        def subsets(n, carry):
            i, j = n // 10, lax.rem(n, 10)
            p0, p1, p2 = (px[i, j, l, cols] for l in range(KP))
            f0, f1, f2 = (p.astype(jnp.float32) for p in (p0, p1, p2))
            f01 = f0 + f1
            zero = jnp.zeros_like(p0)
            entries = (zero, p0, p1, f01, p2, f0 + f2, f1 + f2, f01 + f2)
            for s, value in enumerate(entries):
                s_buf[n * 8 + s, pl.ds(0, cw)] = value.astype(jnp.bfloat16)
            return carry

        lax.fori_loop(1, 99, subsets, 0)

        def row(r, carry):
            i, j = r // 8 + 1, lax.rem(r, 8) + 1
            base = i * 10 + j
            lhs = []
            for nb, d in enumerate((0, -10, 10, -1, 1)):
                at = (base + d) * 8
                parts = []
                for k in range(KP):
                    mask = tab[(r * KP + k) * ST + nb]
                    parts += [s_buf[at + mask, pl.ds(0, cw)], s_buf[at + 7 - mask, pl.ds(0, cw)]]
                lhs.append(jnp.concatenate(parts, axis=0))
            lhs = jnp.concatenate(lhs, axis=1)
            rhs = jnp.concatenate([a_buf[r * ST + nb] for nb in range(ST)], axis=1)
            gathered = lax.dot_general(lhs, rhs, NT, preferred_element_type=jnp.float32).astype(jnp.bfloat16)
            for k in range(KP):
                term[r * KP + k, pl.ds(0, two)] = lax.dot_general(
                    gathered[k * two : (k + 1) * two], px[i, j, k], NT, preferred_element_type=jnp.float32
                )
            return carry

        lax.fori_loop(0, ROWS, row, 0)

        def accumulate(i, total):
            same = tab[OFF_SAME + i].astype(jnp.float32)
            total = total * same + term[tab[OFF_PERM + i], pl.ds(0, two)]
            run[i, pl.ds(0, two)] = total.astype(jnp.bfloat16)
            return total

        lax.fori_loop(0, TASKS, accumulate, jnp.zeros((two, B), jnp.float32))

        def partial(owner):
            some = tab[OFF_SOME + owner].astype(jnp.float32)
            value = run[tab[OFF_LAST + owner], pl.ds(0, two)]
            return (value.astype(jnp.float32) * some).astype(jnp.bfloat16)

        def send_one(i, carry):
            device = offset_device(i)
            send[i] = partial(device[0] * 16 + device[1])
            pltpu.make_async_remote_copy(
                src_ref=send.at[i],
                dst_ref=recv.at[me],
                send_sem=s_sem.at[h],
                recv_sem=r_sem.at[h],
                device_id=device,
                device_id_type=MESH,
            ).start()
            return carry

        lax.fori_loop(1, OWNERS, send_one, 0)
        recv[me] = partial(me)

    for h, (c0, cw) in enumerate(CHUNKS):
        send, recv = sends[h], recvs[h]
        others = pl.ds(0, OWNERS - 1)
        pltpu.make_async_copy(recv.at[others], recv.at[others], r_sem.at[h]).wait()

        def entry(e, carry):
            total = jnp.zeros((cw, B), jnp.float32)
            for q in range(4):
                slot = tab[OFF_INV + e * 4 + q]
                total = total + recv[slot // 2, pl.ds(lax.rem(slot, 2) * cw, cw)].astype(jnp.float32)
            out_ref[e, pl.ds(c0, cw)] = total.astype(jnp.bfloat16)
            return carry

        lax.fori_loop(0, ENTRIES, entry, 0)

    for h in range(n_chunks):
        others = pl.ds(0, OWNERS - 1)
        pltpu.make_async_copy(sends[h].at[others], sends[h].at[others], s_sem.at[h]).wait()


def tables(send_slot, recv_entry):
    slots = send_slot.reshape(TASKS, ST, KP)
    weights = (1 << jnp.arange(KP, dtype=jnp.int32))[None, None, :]
    masks = jnp.sum((1 - slots % 2) * weights, axis=2).reshape(-1)
    owner = slots[:, 0, 0] // 2
    ids = jnp.arange(TASKS, dtype=jnp.int32)
    before = (owner[None, :] < owner[:, None]) | ((owner[None, :] == owner[:, None]) & (ids[None, :] < ids[:, None]))
    rank = jnp.sum(before.astype(jnp.int32), axis=1)
    place = (rank[None, :] == ids[:, None]).astype(jnp.int32)
    perm = jnp.sum(place * ids[None, :], axis=1)
    sorted_owner = jnp.sum(place * owner[None, :], axis=1)
    same = jnp.concatenate([jnp.zeros((1,), jnp.int32), (sorted_owner[1:] == sorted_owner[:-1]).astype(jnp.int32)])
    names = jnp.arange(OWNERS, dtype=jnp.int32)
    upto = jnp.sum((owner[None, :] <= names[:, None]).astype(jnp.int32), axis=1)
    some = jnp.max((owner[None, :] == names[:, None]).astype(jnp.int32), axis=1)
    last = jnp.maximum(upto - 1, 0)
    entries = recv_entry[0]
    at = jnp.arange(2 * OWNERS, dtype=jnp.int32)
    earlier = jnp.sum(((entries[None, :] == entries[:, None]) & (at[None, :] < at[:, None])).astype(jnp.int32), axis=1)
    position = entries * 4 + earlier
    inverse = jnp.sum((position[None, :] == at[:, None]).astype(jnp.int32) * at[None, :], axis=1)
    return jnp.concatenate([masks, perm, same, last, some, inverse])


def body(blocks_a, blocks_p, send_slot, recv_entry):
    tab = tables(send_slot, recv_entry)
    flipped = transposed(blocks_p.reshape(TASKS, B, B), 24).reshape(8, 8, KP, B, B)
    widest = max(cw for _, cw in CHUNKS)
    n_chunks = len(CHUNKS)
    bf16 = jnp.bfloat16
    out = pl.pallas_call(
        galerkin_kernel,
        out_shape=jax.ShapeDtypeStruct((ENTRIES, B, B), bf16),
        in_specs=[
            pl.BlockSpec(memory_space=pltpu.SMEM),
            pl.BlockSpec(memory_space=pl.ANY),
            pl.BlockSpec(memory_space=pl.ANY),
        ],
        out_specs=pl.BlockSpec(memory_space=pltpu.VMEM),
        scratch_shapes=[
            pltpu.VMEM((ROWS * ST, B, B), bf16),
            pltpu.VMEM((10, 10, KP, B, B), bf16),
            pltpu.VMEM((800, widest, B), bf16),
            pltpu.VMEM((TASKS, 2 * widest, B), jnp.float32),
            pltpu.VMEM((TASKS, 2 * widest, B), bf16),
        ]
        + [pltpu.VMEM((OWNERS, 2 * cw, B), bf16) for _, cw in CHUNKS] * 2
        + [
            pltpu.SemaphoreType.DMA,
            pltpu.SemaphoreType.DMA,
            pltpu.SemaphoreType.DMA((4 * n_chunks,)),
            pltpu.SemaphoreType.DMA((4 * n_chunks,)),
            pltpu.SemaphoreType.DMA((n_chunks,)),
            pltpu.SemaphoreType.DMA((n_chunks,)),
        ],
        cost_estimate=pl.CostEstimate(flops=16_000_000_000, bytes_accessed=30_000_000, transcendentals=0),
        compiler_params=pltpu.CompilerParams(
            collective_id=0, has_side_effects=True, vmem_limit_bytes=60 * 2**20
        ),
    )(tab, blocks_a.reshape(ROWS * ST, B, B), flipped)
    return transposed(out, 16)


def solution(mesh):
    in_specs = (
        P("ax", "circ", None, None, None),
        P("ax", "circ", None, None, None),
        P("ax", "circ", None, None, None),
        P(("ax", "circ"), None),
    )
    out_specs = P(("ax", "circ"), None, None)
    return jax.shard_map(body, mesh=mesh, in_specs=in_specs, out_specs=out_specs, check_vma=False)
```

profile of v0, /device:TPU:1, one launch (start us, length us, event | category | flops | bytes accessed | tf_op | source)
XLA Modules:
  0.0 201.7 jit_solution(2713018631841262250)
XLA Ops:
  0.0 0.9 convert_reduce_fusion
  0.9 0.7 multiply_add_fusion
  1.6 0.1 select_reduce_fusion
  1.7 1.0 fusion.6
  2.8 0.2 copy.8
  3.0 0.2 reshape.80
  3.2 1.7 copy.9
  4.9 0.3 reshape.81
  5.2 0.2 convert_reduce_fusion.1
  5.4 0.2 select_reduce_fusion.1
  5.6 0.1 compare_convert_fusion
  5.6 0.1 convert_reduce_fusion.2
  5.8 0.7 concatenate.3.tab
  6.5 0.0 copy-start
  6.5 2.8 %copy-done = bf16[8,8,3,128,128]{4,3,2,1,0:T(8,128)(2,1)S(1)} copy-done((bf16[8,8,3,128,128]{4,3,2,1,0:T(8,128)(2,1)S(1)}, bf16[8,8,3,128,128]{4,3,2,1,0:T(8,128)(2,1)}, u32[]{:S(2)}) %copy-start) | copy-done | bytes 6291480
  9.2 2.1 %shard_map.46 = bf16[192,128,128]{2,1,0:T(8,128)(2,1)S(1)} custom-call(bf16[192,128,128]{2,1,0:T(8,128)(2,1)S(1)} %bitcast.11), custom_call_target="tpu_custom_call" | custom-call | bytes 12582912 | tf_op jit(solution)/shard_map/pallas_call | solution.py:36
  11.4 0.0 copy-start.1
  11.4 2.7 %copy-done.1 = bf16[192,128,128]{2,1,0:T(8,128)(2,1)} copy-done((bf16[192,128,128]{2,1,0:T(8,128)(2,1)}, bf16[192,128,128]{2,1,0:T(8,128)(2,1)S(1)}, u32[]{:S(2)}) %copy-start.1) | copy-done | bytes 6291480
  14.0 183.9 %shard_map.47.x_ref = bf16[64,128,128]{2,1,0:T(8,128)(2,1)} custom-call(s32[1856]{0:T(1024)} %concatenate.3.tab, bf16[320,128,128]{2,1,0:T(8,128)(2,1)} %bitcast.17, bf16[8,8,3,128,128]{4,3,2,1,0:T(8,128)(2,1)} %bitcast.12), custom_call_target="tpu_custom_call" | custom-call | flops 16000000000 | bytes 30000000 | tf_op jit(solution)/shard_map/pallas_call | solution.py:237
  198.0 0.0 copy-start.2
  198.0 1.6 copy-done.2
  199.6 2.2 %shard_map.48 = bf16[64,128,128]{2,1,0:T(8,128)(2,1)} custom-call(bf16[64,128,128]{2,1,0:T(8,128)(2,1)S(1)} %copy-done.2), custom_call_target="tpu_custom_call" | custom-call | bytes 4194304 | tf_op jit(solution)/shard_map/pallas_call | solution.py:36
  (4 shorter events, 0.0 us)
Async XLA Ops:
  6.5 2.8 %copy-start = (bf16[8,8,3,128,128]{4,3,2,1,0:T(8,128)(2,1)S(1)}, bf16[8,8,3,128,128]{4,3,2,1,0:T(8,128)(2,1)}, u32[]{:S(2)}) copy-start(bf16[8,8,3,128,128]{4,3,2,1,0:T(8,128)(2,1)} %param.5) | copy-start | bytes 18874372
  11.4 2.7 %copy-start.1 = (bf16[192,128,128]{2,1,0:T(8,128)(2,1)}, bf16[192,128,128]{2,1,0:T(8,128)(2,1)S(1)}, u32[]{:S(2)}) copy-start(bf16[192,128,128]{2,1,0:T(8,128)(2,1)S(1)} %shard_map.46) | copy-start | bytes 18874372
  198.0 1.6 copy-start.2
where the time goes:
time: 202 us
  Pallas kernels  188 us (93%)
  local copies, waits for them, and re-layouts  10.1 us (5%)
  other arithmetic  3.32 us (2%)
    pallas_call x1, Pallas kernels, body(): pl.pallas_call(galerkin_kernel, out_shape=jax.ShapeDtypeStruct((ENTRIES,...  184 us
    unnamed x7, local copies, waits for them, and re-layouts  8.71 us
    pallas_call x2, Pallas kernels, transposed(): pl.pallas_call(transpose_kernel, grid=(count // step,), out_shape=jax.Sha...  4.28 us

commit v1 on v0

v1 whole, which is shorter than its diff:
```python
import functools

import jax
import jax.numpy as jnp
from jax import lax
from jax.experimental import pallas as pl
from jax.experimental.pallas import tpu as pltpu
from jax.sharding import PartitionSpec as P

MESH = pl.DeviceIdType.MESH
B = 128
ROWS = 64
KP = 3
ST = 5
TASKS = ROWS * KP
OWNERS = 128
ENTRIES = 64
CHUNKS = ((0, 32), (32, 32), (64, 32), (96, 32))
STEP = 37
OFF_PERM = TASKS * ST
OFF_SAME = OFF_PERM + TASKS
OFF_LAST = OFF_SAME + TASKS
OFF_SOME = OFF_LAST + OWNERS
OFF_SRC = OFF_SOME + OWNERS
OFF_WITHIN = OFF_SRC + 2 * OWNERS
BATCH_TASKS = 32
FLIPS = 20


def transpose_kernel(x_ref, o_ref):
    for i in range(x_ref.shape[0]):
        o_ref[i] = x_ref[i].T


def transposed(blocks, step):
    count = blocks.shape[0]
    spec = pl.BlockSpec((step, B, B), lambda i: (i, 0, 0))
    return pl.pallas_call(
        transpose_kernel,
        grid=(count // step,),
        out_shape=jax.ShapeDtypeStruct((count, B, B), jnp.bfloat16),
        in_specs=[spec],
        out_specs=spec,
        cost_estimate=pl.CostEstimate(flops=0, bytes_accessed=count * B * B * 4, transcendentals=0),
        compiler_params=pltpu.CompilerParams(vmem_limit_bytes=62 * 2**20),
    )(blocks)


def offset_device(step):
    ax, ci = lax.axis_index("ax"), lax.axis_index("circ")
    off = lax.rem(step * STEP, 128)
    core = lax.rem(ax + off, 2)
    x = lax.rem(ci + lax.div(off, 2), 4)
    y = lax.rem(lax.div(ci, 4) + lax.div(off, 8), 4)
    z = lax.rem(lax.div(ax, 2) + lax.div(off, 32), 4)
    return z * 2 + core, y * 4 + x


def inner(t):
    return lax.div(t, 6) + 1, lax.rem(t, 6) + 1


def ends(t):
    return 7 * lax.div(t, 8), lax.rem(t, 8)


def sides(t):
    return lax.div(t, 2) + 1, 7 * lax.rem(t, 2)


def galerkin_kernel(tab, a_hbm, p_hbm, out_hbm, out_ref, a_buf, p_buf, px, s_buf, g_buf, run, *rest):
    n_chunks = len(CHUNKS)
    sends, recvs = rest[:n_chunks], rest[n_chunks : 2 * n_chunks]
    a_sem, p_sem, o_sem, hs_sem, hr_sem, s_sem, r_sem = rest[2 * n_chunks :]
    ax, ci = lax.axis_index("ax"), lax.axis_index("circ")
    me = ax * 16 + ci
    n_ax, n_ci = 8, 16

    p_copy = pltpu.make_async_copy(p_hbm, p_buf, p_sem)
    p_copy.start()
    a_copy = pltpu.make_async_copy(a_hbm, a_buf, a_sem)
    a_copy.start()

    barrier = pltpu.get_barrier_semaphore()

    rings = [lax.rem(ax + d, n_ax) for d in range(n_ax)]
    for d in range(1, n_ax):
        pl.semaphore_signal(barrier, inc=1, device_id=(rings[d], ci), device_id_type=MESH)

    def greet(d, carry):
        other = lax.rem(ci + d, n_ci)
        for ring in rings:
            pl.semaphore_signal(barrier, inc=1, device_id=(ring, other), device_id_type=MESH)
        return carry

    lax.fori_loop(1, n_ci, greet, 0)

    p_copy.wait()

    def flip_p(place, count, size):
        def step(n, carry):
            places = [place(n * size + q) for q in range(size)]
            flipped = [p_buf[(i * 8 + j) * KP + k].T for i, j in places for k in range(KP)]
            for q, (i, j) in enumerate(places):
                for k in range(KP):
                    px[i + 1, j + 1, k] = flipped[q * KP + k]
            return carry

        lax.fori_loop(0, count // size, step, 0)

    flip_p(ends, 16, 4)
    flip_p(sides, 12, 4)

    pl.semaphore_wait(barrier, OWNERS - 1)

    up, down = (lax.rem(ax + n_ax - 1, n_ax), ci), (lax.rem(ax + 1, n_ax), ci)
    left, right = (ax, lax.rem(ci + n_ci - 1, n_ci)), (ax, lax.rem(ci + 1, n_ci))
    halos = []
    for h, (c0, cw) in enumerate(CHUNKS):
        cols = pl.ds(c0, cw)
        eight = pl.ds(1, 8)
        four = (
            (px.at[eight, 1, :, cols], px.at[eight, 9, :, cols], left),
            (px.at[eight, 8, :, cols], px.at[eight, 0, :, cols], right),
            (px.at[1, eight, :, cols], px.at[9, eight, :, cols], up),
            (px.at[8, eight, :, cols], px.at[0, eight, :, cols], down),
        )
        copies = []
        for d, (src, dst, device) in enumerate(four):
            copy = pltpu.make_async_remote_copy(
                src_ref=src,
                dst_ref=dst,
                send_sem=hs_sem.at[h * 4 + d],
                recv_sem=hr_sem.at[h * 4 + d],
                device_id=device,
                device_id_type=MESH,
            )
            copy.start()
            copies.append(copy)
        halos.append(copies)

    flip_p(inner, 36, 4)

    a_copy.wait()

    def flip_a(n, carry):
        flipped = [a_buf[n * FLIPS + q].T for q in range(FLIPS)]
        for q in range(FLIPS):
            a_buf[n * FLIPS + q] = flipped[q]
        return carry

    lax.fori_loop(0, ROWS * ST // FLIPS, flip_a, 0)

    for h, (c0, cw) in enumerate(CHUNKS):
        send, recv = sends[h], recvs[h]
        cols = pl.ds(c0, cw)
        two = 2 * cw

        def subsets(i, j):
            n = i * 10 + j
            p0, p1, p2 = (px[i, j, l, cols] for l in range(KP))
            f0, f1, f2 = (p.astype(jnp.float32) for p in (p0, p1, p2))
            f01 = f0 + f1
            zero = jnp.zeros_like(p0)
            entries = (zero, p0, p1, f01, p2, f0 + f2, f1 + f2, f01 + f2)
            for s, value in enumerate(entries):
                s_buf[n * 8 + s, pl.ds(0, cw)] = value.astype(jnp.bfloat16)

        def subsets_own(r, carry):
            subsets(lax.div(r, 8) + 1, lax.rem(r, 8) + 1)
            return carry

        lax.fori_loop(0, ROWS, subsets_own, 0, unroll=2)
        def gather(places):
            sums = []
            for i, j in places:
                r = i * 8 + j
                base = (i + 1) * 10 + j + 1
                lhs = []
                for nb, d in enumerate((0, -10, 10, -1, 1)):
                    at = (base + d) * 8
                    parts = []
                    for k in range(KP):
                        mask = tab[(r * KP + k) * ST + nb]
                        parts += [s_buf[at + mask, pl.ds(0, cw)], s_buf[at + 7 - mask, pl.ds(0, cw)]]
                    lhs.append(jnp.concatenate(parts, axis=0))
                lhs = jnp.concatenate(lhs, axis=1)
                rhs = jnp.concatenate([a_buf[r * ST + nb] for nb in range(ST)], axis=0)
                sums.append(jnp.dot(lhs, rhs, preferred_element_type=jnp.float32).astype(jnp.bfloat16))
            for (i, j), gathered in zip(places, sums):
                for k in range(KP):
                    g_buf[(i * 8 + j) * KP + k, pl.ds(0, two)] = gathered[k * two : (k + 1) * two]

        def batch(place, count, size):
            def step(n, carry):
                gather([place(n * size + q) for q in range(size)])
                return carry

            lax.fori_loop(0, count // size, step, 0)

        batch(inner, 36, 12)

        for copy in halos[h]:
            copy.wait()

        @pl.when(ax == 0)
        def _():
            px[0, pl.ds(1, 8), :, cols] = jnp.zeros((8, KP, cw, B), jnp.bfloat16)

        @pl.when(ax == n_ax - 1)
        def _():
            px[9, pl.ds(1, 8), :, cols] = jnp.zeros((8, KP, cw, B), jnp.bfloat16)

        def subsets_halo(i, carry):
            subsets(i, 0)
            subsets(i, 9)
            subsets(0, i)
            subsets(9, i)
            return carry

        lax.fori_loop(1, 9, subsets_halo, 0)

        batch(ends, 16, 8)
        batch(sides, 12, 12)

        def tasks(step, total):
            terms = []
            blank = jnp.zeros((two, B), jnp.bfloat16)
            for q in range(0, BATCH_TASKS, 2):
                gathered, owned = [], []
                for i in (step * BATCH_TASKS + q, step * BATCH_TASKS + q + 1):
                    gathered.append(g_buf[tab[OFF_PERM + i], pl.ds(0, two)])
                    owned.append(p_buf[tab[OFF_PERM + i]])
                lhs = jnp.concatenate(
                    [
                        jnp.concatenate([gathered[0], blank], axis=1),
                        jnp.concatenate([blank, gathered[1]], axis=1),
                    ],
                    axis=0,
                )
                pair = jnp.dot(lhs, jnp.concatenate(owned, axis=0), preferred_element_type=jnp.float32)
                terms += [pair[:two], pair[two:]]
            values = []
            for q in range(BATCH_TASKS):
                total = total * tab[OFF_SAME + step * BATCH_TASKS + q].astype(jnp.float32) + terms[q]
                values.append(total.astype(jnp.bfloat16))
            for q in range(BATCH_TASKS):
                run[step * BATCH_TASKS + q, pl.ds(0, two)] = values[q]
            return total

        lax.fori_loop(0, TASKS // BATCH_TASKS, tasks, jnp.zeros((two, B), jnp.float32))

        def partial(owner):
            some = tab[OFF_SOME + owner].astype(jnp.float32)
            value = run[tab[OFF_LAST + owner], pl.ds(0, two)]
            return (value.astype(jnp.float32) * some).astype(jnp.bfloat16).reshape(2, cw, B)

        def send_one(i, carry):
            device = offset_device(i)
            send[i] = partial(device[0] * 16 + device[1])
            pltpu.make_async_remote_copy(
                src_ref=send.at[i],
                dst_ref=recv.at[me],
                send_sem=s_sem.at[h],
                recv_sem=r_sem.at[h],
                device_id=device,
                device_id_type=MESH,
            ).start()
            return carry

        lax.fori_loop(1, OWNERS, send_one, 0)
        recv[me] = partial(me)

    outs = []
    for h, (c0, cw) in enumerate(CHUNKS):
        send, recv = sends[h], recvs[h]
        others = pl.ds(0, OWNERS - 1)
        pltpu.make_async_copy(recv.at[others], recv.at[others], r_sem.at[h]).wait()

        def entry(step, carry):
            totals = []
            for q in range(4):
                e = step * 4 + q
                total = jnp.zeros((cw, B), jnp.float32)
                for piece in range(4):
                    source = tab[OFF_SRC + e * 4 + piece]
                    within = tab[OFF_WITHIN + e * 4 + piece]
                    total = total + recv[source, within].astype(jnp.float32)
                totals.append(total.astype(jnp.bfloat16))
            for q in range(4):
                out_ref[step * 4 + q, pl.ds(c0, cw)] = totals[q]
            return carry

        lax.fori_loop(0, ENTRIES // 4, entry, 0)
        done = pltpu.make_async_copy(out_ref.at[:, pl.ds(c0, cw)], out_hbm.at[:, pl.ds(c0, cw)], o_sem.at[h])
        done.start()
        outs.append(done)

    for h in range(n_chunks):
        others = pl.ds(0, OWNERS - 1)
        pltpu.make_async_copy(sends[h].at[others], sends[h].at[others], s_sem.at[h]).wait()
        outs[h].wait()


def tables(send_slot, recv_entry):
    weights = (1 << jnp.arange(KP, dtype=jnp.int32))[None, None, None, None, :]
    masks = jnp.sum((1 - send_slot % 2) * weights, axis=4).reshape(-1)
    owner = (send_slot[:, :, :, 0, 0] // 2).reshape(-1)
    ids = jnp.arange(TASKS, dtype=jnp.int32)
    before = (owner[None, :] < owner[:, None]) | ((owner[None, :] == owner[:, None]) & (ids[None, :] < ids[:, None]))
    rank = jnp.sum(before.astype(jnp.int32), axis=1)
    place = (rank[None, :] == ids[:, None]).astype(jnp.int32)
    perm = jnp.sum(place * ids[None, :], axis=1)
    sorted_owner = jnp.sum(place * owner[None, :], axis=1)
    same = jnp.concatenate([jnp.zeros((1,), jnp.int32), (sorted_owner[1:] == sorted_owner[:-1]).astype(jnp.int32)])
    names = jnp.arange(OWNERS, dtype=jnp.int32)
    upto = jnp.sum((owner[None, :] <= names[:, None]).astype(jnp.int32), axis=1)
    some = jnp.max((owner[None, :] == names[:, None]).astype(jnp.int32), axis=1)
    last = jnp.maximum(upto - 1, 0)
    entries = recv_entry[0]
    at = jnp.arange(2 * OWNERS, dtype=jnp.int32)
    earlier = jnp.sum(((entries[None, :] == entries[:, None]) & (at[None, :] < at[:, None])).astype(jnp.int32), axis=1)
    position = entries * 4 + earlier
    inverse = jnp.sum((position[None, :] == at[:, None]).astype(jnp.int32) * at[None, :], axis=1)
    return jnp.concatenate(
        [masks, perm, same, last, some, inverse // 2, inverse % 2]
    )


def body(blocks_a, blocks_p, send_slot, recv_entry):
    tab = tables(send_slot, recv_entry)
    widest = max(cw for _, cw in CHUNKS)
    n_chunks = len(CHUNKS)
    bf16 = jnp.bfloat16
    out = pl.pallas_call(
        galerkin_kernel,
        out_shape=jax.ShapeDtypeStruct((ENTRIES, B, B), bf16),
        in_specs=[
            pl.BlockSpec(memory_space=pltpu.SMEM),
            pl.BlockSpec(memory_space=pl.ANY),
            pl.BlockSpec(memory_space=pl.ANY),
        ],
        out_specs=pl.BlockSpec(memory_space=pl.ANY),
        scratch_shapes=[
            pltpu.VMEM((ENTRIES, B, B), bf16),
            pltpu.VMEM((ROWS * ST, B, B), bf16),
            pltpu.VMEM((TASKS, B, B), bf16),
            pltpu.VMEM((10, 10, KP, B, B), bf16),
            pltpu.VMEM((800, widest, B), bf16),
            pltpu.VMEM((TASKS, 2 * widest, B), bf16),
            pltpu.VMEM((TASKS, 2 * widest, B), bf16),
        ]
        + [pltpu.VMEM((OWNERS, 2, cw, B), bf16) for _, cw in CHUNKS] * 2
        + [
            pltpu.SemaphoreType.DMA,
            pltpu.SemaphoreType.DMA,
            pltpu.SemaphoreType.DMA((n_chunks,)),
            pltpu.SemaphoreType.DMA((4 * n_chunks,)),
            pltpu.SemaphoreType.DMA((4 * n_chunks,)),
            pltpu.SemaphoreType.DMA((n_chunks,)),
            pltpu.SemaphoreType.DMA((n_chunks,)),
        ],
        cost_estimate=pl.CostEstimate(flops=16_000_000_000, bytes_accessed=30_000_000, transcendentals=0),
        compiler_params=pltpu.CompilerParams(
            collective_id=0, has_side_effects=True, vmem_limit_bytes=60 * 2**20
        ),
    )(tab, blocks_a.reshape(ROWS * ST, B, B), blocks_p.reshape(TASKS, B, B))
    return transposed(out, 16)


def solution(mesh):
    in_specs = (
        P("ax", "circ", None, None, None),
        P("ax", "circ", None, None, None),
        P("ax", "circ", None, None, None),
        P(("ax", "circ"), None),
    )
    out_specs = P(("ax", "circ"), None, None)
    return jax.shard_map(body, mesh=mesh, in_specs=in_specs, out_specs=out_specs, check_vma=False)
```

time: 202 us -> 133 us (0.66)
  Pallas kernels: 188 us -> 128 us
  local copies, waits for them, and re-layouts: 10.1 us -> 2.08 us
    pallas_call x1, Pallas kernels: 184 us -> 124 us  [body(): pl.pallas_call(galerkin_kernel, out_shape=jax.ShapeDtypeStruct((ENTRIES,...]
    unnamed x7 -> x0, local copies, waits for them, and re-layouts: 8.71 us -> none
    pallas_call x2 -> x1, Pallas kernels: 4.28 us -> 4.09 us  [transposed(): pl.pallas_call(transpose_kernel, grid=(count // step,), out_shape=jax.Sha...]
where the time goes in v1:
time: 133 us
  Pallas kernels  128 us (96%)
  other arithmetic  3.33 us (3%)
  local copies, waits for them, and re-layouts  2.08 us (2%)
    pallas_call x1, Pallas kernels, body(): pl.pallas_call(galerkin_kernel, out_shape=jax.ShapeDtypeStruct((ENTRIES,...  124 us
    pallas_call x1, Pallas kernels, transposed(): pl.pallas_call(transpose_kernel, grid=(count // step,), out_shape=jax.Sha...  4.09 us

profile of v1, /device:TPU:1, one launch (start us, length us, event | category | flops | bytes accessed | tf_op | source)
XLA Modules:
  0.0 133.2 jit_solution(13541668889147945206)
XLA Ops:
  0.0 0.9 convert_reduce_fusion
  0.9 0.7 multiply_add_fusion
  1.6 0.1 select_reduce_fusion
  1.8 0.7 slice.9
  2.5 0.1 copy.9
  2.6 0.1 squeeze.4
  2.8 0.2 convert_reduce_fusion.1
  2.9 0.2 select_reduce_fusion.1
  3.1 0.1 compare_convert_fusion
  3.2 0.1 convert_reduce_fusion.2
  3.3 1.0 fusion.6
  4.3 0.2 copy.8
  4.6 0.2 reshape.72
  4.8 0.7 concatenate.3.tab
  5.4 123.6 %shard_map.46.x_ref = bf16[64,128,128]{2,1,0:T(8,128)(2,1)} custom-call(s32[2112]{0:T(1024)} %concatenate.3.tab, bf16[320,128,128]{2,1,0:T(8,128)(2,1)} %bitcast.12, bf16[192,128,128]{2,1,0:T(8,128)(2,1)} %bitcast.13), custom_call_target="tpu_custom_call" | custom-call | flops 16000000000 | bytes 30000000 | tf_op jit(solution)/shard_map/pallas_call | solution.py:335
  129.1 4.1 %shard_map.47 = bf16[64,128,128]{2,1,0:T(8,128)(2,1)} custom-call(bf16[64,128,128]{2,1,0:T(8,128)(2,1)} %shard_map.46.x_ref), custom_call_target="tpu_custom_call" | custom-call | bytes 4194304 | tf_op jit(solution)/shard_map/pallas_call | solution.py:38
  (4 shorter events, 0.0 us)

commit v2 on v1

--- a/solution.py
+++ b/solution.py
@@ -76,10 +76,13 @@
     me = ax * 16 + ci
     n_ax, n_ci = 8, 16
 
-    p_copy = pltpu.make_async_copy(p_hbm, p_buf, p_sem)
-    p_copy.start()
+    p_copies = []
+    for d, (first, count) in enumerate(((0, 8), (56, 8), (8, 24), (32, 24))):
+        part = pl.ds(first * KP, count * KP)
+        copy = pltpu.make_async_copy(p_hbm.at[part], p_buf.at[part], p_sem.at[d])
+        copy.start()
+        p_copies.append(copy)
     a_copy = pltpu.make_async_copy(a_hbm, a_buf, a_sem)
-    a_copy.start()
 
     barrier = pltpu.get_barrier_semaphore()
 
@@ -95,7 +98,9 @@
 
     lax.fori_loop(1, n_ci, greet, 0)
 
-    p_copy.wait()
+    p_copies[0].wait()
+    p_copies[1].wait()
+    a_copy.start()
 
     def flip_p(place, count, size):
         def step(n, carry):
@@ -109,6 +114,8 @@
         lax.fori_loop(0, count // size, step, 0)
 
     flip_p(ends, 16, 4)
+    p_copies[2].wait()
+    p_copies[3].wait()
     flip_p(sides, 12, 4)
 
     pl.semaphore_wait(barrier, OWNERS - 1)
@@ -143,8 +150,21 @@
 
     a_copy.wait()
 
+    def subsets(i, j, cols, cw):
+        n = i * 10 + j
+        p0, p1, p2 = (px[i, j, l, cols] for l in range(KP))
+        f0, f1, f2 = (p.astype(jnp.float32) for p in (p0, p1, p2))
+        f01 = f0 + f1
+        zero = jnp.zeros_like(p0)
+        entries = (zero, p0, p1, f01, p2, f0 + f2, f1 + f2, f01 + f2)
+        for s, value in enumerate(entries):
+            s_buf[n * 8 + s, pl.ds(0, cw)] = value.astype(jnp.bfloat16)
+
     def flip_a(n, carry):
         flipped = [a_buf[n * FLIPS + q].T for q in range(FLIPS)]
+        for q in range(4):
+            r = n * 4 + q
+            subsets(lax.div(r, 8) + 1, lax.rem(r, 8) + 1, pl.ds(*CHUNKS[0]), CHUNKS[0][1])
         for q in range(FLIPS):
             a_buf[n * FLIPS + q] = flipped[q]
         return carry
@@ -156,21 +176,13 @@
         cols = pl.ds(c0, cw)
         two = 2 * cw
 
-        def subsets(i, j):
-            n = i * 10 + j
-            p0, p1, p2 = (px[i, j, l, cols] for l in range(KP))
-            f0, f1, f2 = (p.astype(jnp.float32) for p in (p0, p1, p2))
-            f01 = f0 + f1
-            zero = jnp.zeros_like(p0)
-            entries = (zero, p0, p1, f01, p2, f0 + f2, f1 + f2, f01 + f2)
-            for s, value in enumerate(entries):
-                s_buf[n * 8 + s, pl.ds(0, cw)] = value.astype(jnp.bfloat16)
-
         def subsets_own(r, carry):
-            subsets(lax.div(r, 8) + 1, lax.rem(r, 8) + 1)
-            return carry
-
-        lax.fori_loop(0, ROWS, subsets_own, 0, unroll=2)
+            subsets(lax.div(r, 8) + 1, lax.rem(r, 8) + 1, cols, cw)
+            return carry
+
+        if h > 0:
+            lax.fori_loop(0, ROWS, subsets_own, 0, unroll=2)
+
         def gather(places):
             sums = []
             for i, j in places:
@@ -212,10 +224,10 @@
             px[9, pl.ds(1, 8), :, cols] = jnp.zeros((8, KP, cw, B), jnp.bfloat16)
 
         def subsets_halo(i, carry):
-            subsets(i, 0)
-            subsets(i, 9)
-            subsets(0, i)
-            subsets(9, i)
+            subsets(i, 0, cols, cw)
+            subsets(i, 9, cols, cw)
+            subsets(0, i, cols, cw)
+            subsets(9, i, cols, cw)
             return carry
 
         lax.fori_loop(1, 9, subsets_halo, 0)
@@ -319,8 +331,9 @@
     last = jnp.maximum(upto - 1, 0)
     entries = recv_entry[0]
     at = jnp.arange(2 * OWNERS, dtype=jnp.int32)
-    earlier = jnp.sum(((entries[None, :] == entries[:, None]) & (at[None, :] < at[:, None])).astype(jnp.int32), axis=1)
-    position = entries * 4 + earlier
+    same_entry = (entries[None, :] == entries[:, None]) & (at[None, :] < at[:, None])
+    own_entry = jnp.where(at[None, :] == at[:, None], 4 * entries[None, :], 0)
+    position = jnp.sum(same_entry.astype(jnp.int32) + own_entry, axis=1)
     inverse = jnp.sum((position[None, :] == at[:, None]).astype(jnp.int32) * at[None, :], axis=1)
     return jnp.concatenate(
         [masks, perm, same, last, some, inverse // 2, inverse % 2]
@@ -353,7 +366,7 @@
         + [pltpu.VMEM((OWNERS, 2, cw, B), bf16) for _, cw in CHUNKS] * 2
         + [
             pltpu.SemaphoreType.DMA,
-            pltpu.SemaphoreType.DMA,
+            pltpu.SemaphoreType.DMA((4,)),
             pltpu.SemaphoreType.DMA((n_chunks,)),
             pltpu.SemaphoreType.DMA((4 * n_chunks,)),
             pltpu.SemaphoreType.DMA((4 * n_chunks,)),
@@ -365,7 +378,7 @@
             collective_id=0, has_side_effects=True, vmem_limit_bytes=60 * 2**20
         ),
     )(tab, blocks_a.reshape(ROWS * ST, B, B), blocks_p.reshape(TASKS, B, B))
-    return transposed(out, 16)
+    return transposed(out, 32)
 
 
 def solution(mesh):

time: 133 us -> 132 us (level)
  Pallas kernels: 128 us -> 126 us
where the time goes in v2:
time: 132 us
  Pallas kernels  126 us (95%)
  other arithmetic  3.33 us (3%)
  local copies, waits for them, and re-layouts  2.08 us (2%)
    pallas_call x1, Pallas kernels, body(): pl.pallas_call(galerkin_kernel, out_shape=jax.ShapeDtypeStruct((ENTRIES,...  124 us
    pallas_call x1, Pallas kernels, transposed(): pl.pallas_call(transpose_kernel, grid=(count // step,), out_shape=jax.Sha...  2.87 us

profile of v2, /device:TPU:1, one launch (start us, length us, event | category | flops | bytes accessed | tf_op | source)
XLA Modules:
  0.0 131.9 jit_solution(10311126926917484269)
XLA Ops:
  0.0 0.7 broadcast_multiply_fusion
  0.7 0.9 add_reduce_fusion
  1.6 0.1 select_reduce_fusion
  1.8 0.7 slice.9
  2.5 0.1 copy.9
  2.6 0.1 squeeze.3
  2.8 0.2 convert_reduce_fusion
  2.9 0.2 select_reduce_fusion.1
  3.1 0.1 compare_convert_fusion
  3.2 0.1 convert_reduce_fusion.1
  3.3 1.0 fusion.6
  4.3 0.2 copy.8
  4.6 0.2 reshape.72
  4.8 0.7 concatenate.3.tab
  5.4 123.6 %shard_map.46.x_ref = bf16[64,128,128]{2,1,0:T(8,128)(2,1)} custom-call(s32[2112]{0:T(1024)} %concatenate.3.tab, bf16[320,128,128]{2,1,0:T(8,128)(2,1)} %bitcast.10, bf16[192,128,128]{2,1,0:T(8,128)(2,1)} %bitcast.11), custom_call_target="tpu_custom_call" | custom-call | flops 16000000000 | bytes 30000000 | tf_op jit(solution)/shard_map/pallas_call | solution.py:348
  129.0 2.9 %shard_map.47 = bf16[64,128,128]{2,1,0:T(8,128)(2,1)} custom-call(bf16[64,128,128]{2,1,0:T(8,128)(2,1)} %shard_map.46.x_ref), custom_call_target="tpu_custom_call" | custom-call | bytes 4194304 | tf_op jit(solution)/shard_map/pallas_call | solution.py:38
  (4 shorter events, 0.0 us)

commit v3 on v2

--- a/solution.py
+++ b/solution.py
@@ -17,7 +17,7 @@
 ENTRIES = 64
 CHUNKS = ((0, 32), (32, 32), (64, 32), (96, 32))
 STEP = 37
-OFF_PERM = TASKS * ST
+OFF_PERM = 0
 OFF_SAME = OFF_PERM + TASKS
 OFF_LAST = OFF_SAME + TASKS
 OFF_SOME = OFF_LAST + OWNERS
@@ -68,7 +68,7 @@
     return lax.div(t, 2) + 1, 7 * lax.rem(t, 2)
 
 
-def galerkin_kernel(tab, a_hbm, p_hbm, out_hbm, out_ref, a_buf, p_buf, px, s_buf, g_buf, run, *rest):
+def galerkin_kernel(picks, tab, a_hbm, p_hbm, out_hbm, out_ref, a_buf, p_buf, px, s_buf, g_buf, run, *rest):
     n_chunks = len(CHUNKS)
     sends, recvs = rest[:n_chunks], rest[n_chunks : 2 * n_chunks]
     a_sem, p_sem, o_sem, hs_sem, hr_sem, s_sem, r_sem = rest[2 * n_chunks :]
@@ -193,7 +193,7 @@
                     at = (base + d) * 8
                     parts = []
                     for k in range(KP):
-                        mask = tab[(r * KP + k) * ST + nb]
+                        mask = picks[(r * KP + k) * ST + nb]
                         parts += [s_buf[at + mask, pl.ds(0, cw)], s_buf[at + 7 - mask, pl.ds(0, cw)]]
                     lhs.append(jnp.concatenate(parts, axis=0))
                 lhs = jnp.concatenate(lhs, axis=1)
@@ -335,13 +335,13 @@
     own_entry = jnp.where(at[None, :] == at[:, None], 4 * entries[None, :], 0)
     position = jnp.sum(same_entry.astype(jnp.int32) + own_entry, axis=1)
     inverse = jnp.sum((position[None, :] == at[:, None]).astype(jnp.int32) * at[None, :], axis=1)
-    return jnp.concatenate(
-        [masks, perm, same, last, some, inverse // 2, inverse % 2]
+    return masks, jnp.concatenate(
+        [perm, same, last, some, inverse // 2, inverse % 2]
     )
 
 
 def body(blocks_a, blocks_p, send_slot, recv_entry):
-    tab = tables(send_slot, recv_entry)
+    picks, tab = tables(send_slot, recv_entry)
     widest = max(cw for _, cw in CHUNKS)
     n_chunks = len(CHUNKS)
     bf16 = jnp.bfloat16
@@ -349,6 +349,7 @@
         galerkin_kernel,
         out_shape=jax.ShapeDtypeStruct((ENTRIES, B, B), bf16),
         in_specs=[
+            pl.BlockSpec(memory_space=pltpu.SMEM),
             pl.BlockSpec(memory_space=pltpu.SMEM),
             pl.BlockSpec(memory_space=pl.ANY),
             pl.BlockSpec(memory_space=pl.ANY),
@@ -377,8 +378,8 @@
         compiler_params=pltpu.CompilerParams(
             collective_id=0, has_side_effects=True, vmem_limit_bytes=60 * 2**20
         ),
-    )(tab, blocks_a.reshape(ROWS * ST, B, B), blocks_p.reshape(TASKS, B, B))
-    return transposed(out, 32)
+    )(picks, tab, blocks_a.reshape(ROWS * ST, B, B), blocks_p.reshape(TASKS, B, B))
+    return transposed(out, 64)
 
 
 def solution(mesh):

time: 132 us -> 133 us (level)
  no operation moved by 1% of the time
where the time goes in v3:
time: 133 us
  Pallas kernels  127 us (95%)
  other arithmetic  3.33 us (3%)
  local copies, waits for them, and re-layouts  2.68 us (2%)
    pallas_call x1, Pallas kernels, body(): pl.pallas_call(galerkin_kernel, out_shape=jax.ShapeDtypeStruct((ENTRIES,...  124 us
    pallas_call x1, Pallas kernels, transposed(): pl.pallas_call(transpose_kernel, grid=(count // step,), out_shape=jax.Sha...  3.5 us

profile of v3, /device:TPU:1, one launch (start us, length us, event | category | flops | bytes accessed | tf_op | source)
XLA Modules:
  0.0 133.1 jit_solution(2114108327176030540)
XLA Ops:
  0.0 0.7 broadcast_multiply_fusion
  0.7 0.9 add_reduce_fusion
  1.6 0.1 select_reduce_fusion
  1.8 0.7 slice.9
  2.5 0.1 copy.9
  2.6 0.1 squeeze.3
  2.8 0.2 convert_reduce_fusion
  2.9 0.2 select_reduce_fusion.1
  3.1 0.1 compare_convert_fusion
  3.2 0.1 convert_reduce_fusion.1
  3.3 0.7 concatenate.3.tab
  4.0 1.0 fusion.6
  5.0 0.2 copy.8
  5.2 0.8 reshape.72.picks
  6.0 123.6 %shard_map.46.x_ref = bf16[64,128,128]{2,1,0:T(8,128)(2,1)} custom-call(s32[960]{0:T(1024)} %reshape.72.picks, s32[1152]{0:T(1024)} %concatenate.3.tab, bf16[320,128,128]{2,1,0:T(8,128)(2,1)} %bitcast.10, bf16[192,128,128]{2,1,0:T(8,128)(2,1)} %bitcast.11), custom_call_target="tpu_custom_call" | custom-call | flops 16000000000 | bytes 30000000 | tf_op jit(solution)/shard_map/pallas_call | solution.py:348
  129.6 3.5 %shard_map.47 = bf16[64,128,128]{2,1,0:T(8,128)(2,1)} custom-call(bf16[64,128,128]{2,1,0:T(8,128)(2,1)} %shard_map.46.x_ref), custom_call_target="tpu_custom_call" | custom-call | bytes 4194304 | tf_op jit(solution)/shard_map/pallas_call | solution.py:38
  (4 shorter events, 0.0 us)
